TPU v7x, 32 devices: a whole 2x2x4 slice. The times are simulated.
32 devices in a mesh: row: 8 (over z, core), col: 4 (over y, x).
Axes of the slice: x: 2, y: 2, z: 4, core: 2. Of those that a mesh axis runs over, the one named last changes fastest.
Arguments:
- matrix: float32 [4, 1024, 8, 512], P(None, 'row', None, 'col'), may hold values from 0 to 11, as said below
Outputs:
- factored: float32 [4, 1024, 8, 512], P(None, 'row', None, 'col')
Inputs may be any that keep to these rules, and one draw needn't show every extreme that they name: matrix is symmetric and positive definite.
All inputs are finite; a program needn't handle non-finite values.
Results may differ from a plain program's by a relative error of at most 0.0003.
Values sent between devices are 32-bit elements; how exact they have to be, the bound alone decides.
A program may use at most 64 MiB of HBM per device.

v0:
```python
import jax
import jax.numpy as jnp
from jax import lax
from jax.sharding import PartitionSpec as P

PANELS = 2


def from_root(block, axis, owner):
    block = jnp.where(lax.axis_index(axis) == owner, block, jnp.zeros_like(block))
    return lax.psum(block, axis)


def body(matrix):
    rows_n = lax.axis_size("row")
    cols_n = lax.axis_size("col")
    row_at = lax.axis_index("row")
    col_at = lax.axis_index("col")
    tiles_r, width, tiles_c, _ = matrix.shape
    row_tile = jnp.arange(tiles_r, dtype=jnp.int32) * rows_n + row_at
    col_tile = jnp.arange(tiles_c, dtype=jnp.int32) * cols_n + col_at
    identity = jnp.eye(width, dtype=jnp.float32)
    work = matrix
    for panel in range(PANELS):
        slot_r = panel // rows_n
        owner_r = panel % rows_n
        factor_slot_c = panel // cols_n
        factor_owner_c = panel % cols_n
        diag = from_root(work[slot_r, :, factor_slot_c, :], "row", owner_r)
        diag = jnp.where(col_at == factor_owner_c, diag, identity)
        factor_tile = jnp.linalg.cholesky(diag)
        column = work[:, :, factor_slot_c, :].reshape(tiles_r * width, width)
        solved = lax.linalg.triangular_solve(
            factor_tile, column, left_side=False, lower=True, transpose_a=True
        ).reshape(tiles_r, width, width)
        placed = row_tile[:, None, None]
        local_panel = jnp.where(
            placed > panel, solved, jnp.where(placed == panel, factor_tile[None], 0.0)
        )
        factor_row_panel = from_root(local_panel, "col", factor_owner_c)

        def fetch(slot, gathered):
            tile_id = slot * cols_n + col_at
            source = lax.dynamic_index_in_dim(
                factor_row_panel, tile_id // rows_n, 0, keepdims=False
            )
            arrived = from_root(source, "row", tile_id % rows_n)
            return lax.dynamic_update_index_in_dim(gathered, arrived, slot, 0)

        factor_col_panel = lax.fori_loop(
            0, tiles_c, fetch, jnp.zeros((tiles_c, width, width), jnp.float32)
        )
        trimmed_rows_use = jnp.where(row_tile[:, None, None] > panel, factor_row_panel, 0.0)
        trimmed_cols_use = jnp.where(col_tile[:, None, None] > panel, factor_col_panel, 0.0)
        update = jnp.einsum(
            "tab,sqb->tasq", trimmed_rows_use, trimmed_cols_use, precision=lax.Precision.HIGHEST
        )
        work = work - update
        slot_c = panel // cols_n
        owner_c = panel % cols_n
        current = work[:, :, slot_c, :]
        fresh = jnp.where(col_at == owner_c, factor_row_panel, current)
        work = work.at[:, :, slot_c, :].set(fresh)
    lane = jnp.arange(width, dtype=jnp.int32)
    global_row = row_tile[:, None, None, None] * width + lane[None, :, None, None]
    global_col = col_tile[None, None, :, None] * width + lane[None, None, None, :]
    return jnp.where(global_row >= global_col, work, 0.0)


def solution(mesh):
    placed = (P(None, "row", None, "col"),)
    return jax.shard_map(
        body, mesh=mesh, in_specs=placed, out_specs=P(None, "row", None, "col"), check_vma=False
    )
```

profile of v0, /device:TPU:29, one launch (start us, length us, event | category | flops | bytes accessed | tf_op | source)
XLA Modules:
  0.0 1170.6 jit_solution(2797137284923018499)
XLA Ops:
  6.5 1.1 slice.76
  8.6 1.7 slice.77
  10.3 51.4 %all-reduce.7.cloned.1.call-done = f32[128,128]{0,1:T(8,128)} async-done(((f32[128,128]{0,1:T(8,128)}), f32[128,128]{0,1:T(8,128)}) %all-reduce.7.cloned.1.call-update) | async-done | bytes 65552 | tf_op jit(solution)/shard_map/psum | solution.py:11
  61.8 11.7 %cholesky.44 = f32[128,128]{1,0:T(8,128)S(1)} custom-call(f32[128,128]{1,0:T(8,128)S(1)} %fusion.24), custom_call_target="Cholesky" | custom-call | tf_op jit(solution)/shard_map/jit(cholesky)/cholesky | solution.py:31
  74.9 9.8 custom-call.6
  86.3 1.8 copy.22
  88.2 42.2 %all-reduce.9.cloned.1.call-done = f32[4,128,128]{1,2,0:T(8,128)} async-done(((f32[4,128,128]{1,2,0:T(8,128)}), f32[4,128,128]{1,2,0:T(8,128)}) %all-reduce.9.cloned.1.call-update) | async-done | bytes 262160 | tf_op jit(solution)/shard_map/psum | solution.py:11
  130.4 450.5 %while.32 = (s32[]{:T(128)}, f32[8,128,128]{2,1,0:T(8,128)S(1)}, s32[]{:T(128)}, f32[4,128,128]{1,2,0:T(8,128)}, s32[]{:T(128)}, /*index=5*/s32[]{:T(128)}, s32[...) while((s32[]{:T(128)}, f32[8,128,128]{2,1,0:T(8,128)S(1)}, ...), condition=%wide.region_6.9_spmd, body=%wide.region_4.8_spmd.sunk | while | flops 32798 | bytes 917972 | solution.py:50
  130.5 0.8 constant_dynamic-slice_fusion.4
  132.2 53.0 %all-reduce.15.cloned.1.call-done = f32[1,128,128]{2,1,0:T(8,128)} async-done(((f32[1,128,128]{2,1,0:T(8,128)}), f32[1,128,128]{2,1,0:T(8,128)}) %all-reduce.15.cloned.1.call-update) | async-done | bytes 65552 | tf_op jit(solution)/shard_map/while/body/eval_jaxpr/psum | solution.py:11
  185.2 0.8 constant_dynamic-update-slice_fusion.4
  187.7 53.8 %all-reduce.15.cloned.1.call-done = f32[1,128,128]{2,1,0:T(8,128)} async-done(((f32[1,128,128]{2,1,0:T(8,128)}), f32[1,128,128]{2,1,0:T(8,128)}) %all-reduce.15.cloned.1.call-update) | async-done | bytes 65552 | tf_op jit(solution)/shard_map/while/body/eval_jaxpr/psum | solution.py:11
  241.5 0.8 constant_dynamic-update-slice_fusion.4
  243.9 53.8 %all-reduce.15.cloned.1.call-done = f32[1,128,128]{2,1,0:T(8,128)} async-done(((f32[1,128,128]{2,1,0:T(8,128)}), f32[1,128,128]{2,1,0:T(8,128)}) %all-reduce.15.cloned.1.call-update) | async-done | bytes 65552 | tf_op jit(solution)/shard_map/while/body/eval_jaxpr/psum | solution.py:11
  297.8 0.8 constant_dynamic-update-slice_fusion.4
  300.2 53.8 %all-reduce.15.cloned.1.call-done = f32[1,128,128]{2,1,0:T(8,128)} async-done(((f32[1,128,128]{2,1,0:T(8,128)}), f32[1,128,128]{2,1,0:T(8,128)}) %all-reduce.15.cloned.1.call-update) | async-done | bytes 65552 | tf_op jit(solution)/shard_map/while/body/eval_jaxpr/psum | solution.py:11
  354.1 0.8 constant_dynamic-update-slice_fusion.4
  356.5 54.1 %all-reduce.15.cloned.1.call-done = f32[1,128,128]{2,1,0:T(8,128)} async-done(((f32[1,128,128]{2,1,0:T(8,128)}), f32[1,128,128]{2,1,0:T(8,128)}) %all-reduce.15.cloned.1.call-update) | async-done | bytes 65552 | tf_op jit(solution)/shard_map/while/body/eval_jaxpr/psum | solution.py:11
  410.7 0.8 constant_dynamic-update-slice_fusion.4
  413.1 54.1 %all-reduce.15.cloned.1.call-done = f32[1,128,128]{2,1,0:T(8,128)} async-done(((f32[1,128,128]{2,1,0:T(8,128)}), f32[1,128,128]{2,1,0:T(8,128)}) %all-reduce.15.cloned.1.call-update) | async-done | bytes 65552 | tf_op jit(solution)/shard_map/while/body/eval_jaxpr/psum | solution.py:11
  467.3 0.8 constant_dynamic-update-slice_fusion.4
  469.7 54.1 %all-reduce.15.cloned.1.call-done = f32[1,128,128]{2,1,0:T(8,128)} async-done(((f32[1,128,128]{2,1,0:T(8,128)}), f32[1,128,128]{2,1,0:T(8,128)}) %all-reduce.15.cloned.1.call-update) | async-done | bytes 65552 | tf_op jit(solution)/shard_map/while/body/eval_jaxpr/psum | solution.py:11
  523.8 0.8 constant_dynamic-update-slice_fusion.4
  526.3 53.8 %all-reduce.15.cloned.1.call-done = f32[1,128,128]{2,1,0:T(8,128)} async-done(((f32[1,128,128]{2,1,0:T(8,128)}), f32[1,128,128]{2,1,0:T(8,128)}) %all-reduce.15.cloned.1.call-update) | async-done | bytes 65552 | tf_op jit(solution)/shard_map/while/body/eval_jaxpr/psum | solution.py:11
  580.1 0.8 constant_dynamic-update-slice_fusion.4
  581.0 3.6 convolution_subtract_fusion.1
  585.7 52.4 %all-reduce.11.cloned.1.call-done = f32[128,128]{0,1:T(8,128)} async-done(((f32[128,128]{0,1:T(8,128)}), f32[128,128]{0,1:T(8,128)}) %all-reduce.11.cloned.1.call-update) | async-done | bytes 65552 | tf_op jit(solution)/shard_map/psum | solution.py:11
  638.2 11.7 %cholesky.55 = f32[128,128]{1,0:T(8,128)S(1)} custom-call(f32[128,128]{1,0:T(8,128)S(1)} %fusion.22), custom_call_target="Cholesky" | custom-call | tf_op jit(solution)/shard_map/jit(cholesky)/cholesky | solution.py:31
  651.3 9.8 custom-call.7
  662.7 44.8 %all-reduce.13.cloned.1.call-done = f32[4,128,128]{1,2,0:T(8,128)} async-done(((f32[4,128,128]{1,2,0:T(8,128)}), f32[4,128,128]{1,2,0:T(8,128)}) %all-reduce.13.cloned.1.call-update) | async-done | bytes 262160 | tf_op jit(solution)/shard_map/psum | solution.py:11
  707.6 450.8 %while.33 = (s32[]{:T(128)}, f32[8,128,128]{2,1,0:T(8,128)S(1)}, s32[]{:T(128)}, f32[4,128,128]{1,2,0:T(8,128)}, s32[]{:T(128)}, /*index=5*/s32[]{:T(128)}, s32[...) while((s32[]{:T(128)}, f32[8,128,128]{2,1,0:T(8,128)S(1)}, ...), condition=%wide.region_11.14_spmd, body=%wide.region_9.13_spmd.sunk | while | flops 32798 | bytes 917972 | solution.py:50
  707.7 0.8 constant_dynamic-slice_fusion.5
  709.3 53.1 %all-reduce.17.cloned.1.call-done = f32[1,128,128]{2,1,0:T(8,128)} async-done(((f32[1,128,128]{2,1,0:T(8,128)}), f32[1,128,128]{2,1,0:T(8,128)}) %all-reduce.17.cloned.1.call-update) | async-done | bytes 65552 | tf_op jit(solution)/shard_map/while/body/eval_jaxpr/psum | solution.py:11
  762.5 0.8 constant_dynamic-update-slice_fusion.5
  764.9 53.9 %all-reduce.17.cloned.1.call-done = f32[1,128,128]{2,1,0:T(8,128)} async-done(((f32[1,128,128]{2,1,0:T(8,128)}), f32[1,128,128]{2,1,0:T(8,128)}) %all-reduce.17.cloned.1.call-update) | async-done | bytes 65552 | tf_op jit(solution)/shard_map/while/body/eval_jaxpr/psum | solution.py:11
  818.9 0.8 constant_dynamic-update-slice_fusion.5
  821.3 54.0 %all-reduce.17.cloned.1.call-done = f32[1,128,128]{2,1,0:T(8,128)} async-done(((f32[1,128,128]{2,1,0:T(8,128)}), f32[1,128,128]{2,1,0:T(8,128)}) %all-reduce.17.cloned.1.call-update) | async-done | bytes 65552 | tf_op jit(solution)/shard_map/while/body/eval_jaxpr/psum | solution.py:11
  875.3 0.8 constant_dynamic-update-slice_fusion.5
  877.8 53.9 %all-reduce.17.cloned.1.call-done = f32[1,128,128]{2,1,0:T(8,128)} async-done(((f32[1,128,128]{2,1,0:T(8,128)}), f32[1,128,128]{2,1,0:T(8,128)}) %all-reduce.17.cloned.1.call-update) | async-done | bytes 65552 | tf_op jit(solution)/shard_map/while/body/eval_jaxpr/psum | solution.py:11
  931.7 0.8 constant_dynamic-update-slice_fusion.5
  934.2 53.9 %all-reduce.17.cloned.1.call-done = f32[1,128,128]{2,1,0:T(8,128)} async-done(((f32[1,128,128]{2,1,0:T(8,128)}), f32[1,128,128]{2,1,0:T(8,128)}) %all-reduce.17.cloned.1.call-update) | async-done | bytes 65552 | tf_op jit(solution)/shard_map/while/body/eval_jaxpr/psum | solution.py:11
  988.1 0.8 constant_dynamic-update-slice_fusion.5
  990.6 53.9 %all-reduce.17.cloned.1.call-done = f32[1,128,128]{2,1,0:T(8,128)} async-done(((f32[1,128,128]{2,1,0:T(8,128)}), f32[1,128,128]{2,1,0:T(8,128)}) %all-reduce.17.cloned.1.call-update) | async-done | bytes 65552 | tf_op jit(solution)/shard_map/while/body/eval_jaxpr/psum | solution.py:11
  1044.5 0.8 constant_dynamic-update-slice_fusion.5
  1047.0 54.2 %all-reduce.17.cloned.1.call-done = f32[1,128,128]{2,1,0:T(8,128)} async-done(((f32[1,128,128]{2,1,0:T(8,128)}), f32[1,128,128]{2,1,0:T(8,128)}) %all-reduce.17.cloned.1.call-update) | async-done | bytes 65552 | tf_op jit(solution)/shard_map/while/body/eval_jaxpr/psum | solution.py:11
  1103.7 53.9 %all-reduce.17.cloned.1.call-done = f32[1,128,128]{2,1,0:T(8,128)} async-done(((f32[1,128,128]{2,1,0:T(8,128)}), f32[1,128,128]{2,1,0:T(8,128)}) %all-reduce.17.cloned.1.call-update) | async-done | bytes 65552 | tf_op jit(solution)/shard_map/while/body/eval_jaxpr/psum | solution.py:11
  1158.4 3.0 convolution_subtract_fusion
  1161.9 1.8 copy.32
  (134 shorter events, 34.1 us)
Async XLA Ops:
  6.5 55.1 %all-reduce.7.cloned.1.call-start = ((), (), s32[]{:S(2)}) async-start(), calls=%async_computation | async-start | bytes 131072 | tf_op jit(solution)/shard_map/psum | solution.py:11
  7.6 78.7 %copy-start = (f32[4,128,8,128]{3,2,1,0:T(8,128)S(1)}, f32[4,128,8,128]{3,2,1,0:T(8,128)}, u32[]{:S(2)}) copy-start(f32[4,128,8,128]{3,2,1,0:T(8,128)} %param.12) | copy-start | bytes 6291460
  8.4 122.0 %all-reduce.9.cloned.1.call-start = ((), (), s32[]{:S(2)}) async-start(), calls=%async_computation.1 | async-start | bytes 524288 | tf_op jit(solution)/shard_map/psum | solution.py:11
  130.5 54.7 %all-reduce.15.cloned.1.call-start = ((), (), s32[]{:S(2)}) async-start(), calls=%async_computation.4 | async-start | bytes 131072 | tf_op jit(solution)/shard_map/while/body/eval_jaxpr/psum | solution.py:11
  186.0 55.4 %all-reduce.15.cloned.1.call-start = ((), (), s32[]{:S(2)}) async-start(), calls=%async_computation.4 | async-start | bytes 131072 | tf_op jit(solution)/shard_map/while/body/eval_jaxpr/psum | solution.py:11
  242.3 55.5 %all-reduce.15.cloned.1.call-start = ((), (), s32[]{:S(2)}) async-start(), calls=%async_computation.4 | async-start | bytes 131072 | tf_op jit(solution)/shard_map/while/body/eval_jaxpr/psum | solution.py:11
  298.6 55.4 %all-reduce.15.cloned.1.call-start = ((), (), s32[]{:S(2)}) async-start(), calls=%async_computation.4 | async-start | bytes 131072 | tf_op jit(solution)/shard_map/while/body/eval_jaxpr/psum | solution.py:11
  354.9 55.8 %all-reduce.15.cloned.1.call-start = ((), (), s32[]{:S(2)}) async-start(), calls=%async_computation.4 | async-start | bytes 131072 | tf_op jit(solution)/shard_map/while/body/eval_jaxpr/psum | solution.py:11
  411.5 55.8 %all-reduce.15.cloned.1.call-start = ((), (), s32[]{:S(2)}) async-start(), calls=%async_computation.4 | async-start | bytes 131072 | tf_op jit(solution)/shard_map/while/body/eval_jaxpr/psum | solution.py:11
  468.1 55.7 %all-reduce.15.cloned.1.call-start = ((), (), s32[]{:S(2)}) async-start(), calls=%async_computation.4 | async-start | bytes 131072 | tf_op jit(solution)/shard_map/while/body/eval_jaxpr/psum | solution.py:11
  524.7 55.4 %all-reduce.15.cloned.1.call-start = ((), (), s32[]{:S(2)}) async-start(), calls=%async_computation.4 | async-start | bytes 131072 | tf_op jit(solution)/shard_map/while/body/eval_jaxpr/psum | solution.py:11
  581.0 57.1 %all-reduce.11.cloned.1.call-start = ((), (), s32[]{:S(2)}) async-start(), calls=%async_computation.2 | async-start | bytes 131072 | tf_op jit(solution)/shard_map/psum | solution.py:11
  581.0 3.6 copy-start.2
  585.3 122.3 %all-reduce.13.cloned.1.call-start = ((), (), s32[]{:S(2)}) async-start(), calls=%async_computation.3 | async-start | bytes 524288 | tf_op jit(solution)/shard_map/psum | solution.py:11
  707.6 54.9 %all-reduce.17.cloned.1.call-start = ((), (), s32[]{:S(2)}) async-start(), calls=%async_computation.5 | async-start | bytes 131072 | tf_op jit(solution)/shard_map/while/body/eval_jaxpr/psum | solution.py:11
  763.3 55.6 %all-reduce.17.cloned.1.call-start = ((), (), s32[]{:S(2)}) async-start(), calls=%async_computation.5 | async-start | bytes 131072 | tf_op jit(solution)/shard_map/while/body/eval_jaxpr/psum | solution.py:11
  819.7 55.6 %all-reduce.17.cloned.1.call-start = ((), (), s32[]{:S(2)}) async-start(), calls=%async_computation.5 | async-start | bytes 131072 | tf_op jit(solution)/shard_map/while/body/eval_jaxpr/psum | solution.py:11
  876.1 55.6 %all-reduce.17.cloned.1.call-start = ((), (), s32[]{:S(2)}) async-start(), calls=%async_computation.5 | async-start | bytes 131072 | tf_op jit(solution)/shard_map/while/body/eval_jaxpr/psum | solution.py:11
  932.5 55.5 %all-reduce.17.cloned.1.call-start = ((), (), s32[]{:S(2)}) async-start(), calls=%async_computation.5 | async-start | bytes 131072 | tf_op jit(solution)/shard_map/while/body/eval_jaxpr/psum | solution.py:11
  988.9 55.6 %all-reduce.17.cloned.1.call-start = ((), (), s32[]{:S(2)}) async-start(), calls=%async_computation.5 | async-start | bytes 131072 | tf_op jit(solution)/shard_map/while/body/eval_jaxpr/psum | solution.py:11
  1045.3 55.9 %all-reduce.17.cloned.1.call-start = ((), (), s32[]{:S(2)}) async-start(), calls=%async_computation.5 | async-start | bytes 131072 | tf_op jit(solution)/shard_map/while/body/eval_jaxpr/psum | solution.py:11
  1102.1 55.5 %all-reduce.17.cloned.1.call-start = ((), (), s32[]{:S(2)}) async-start(), calls=%async_computation.5 | async-start | bytes 131072 | tf_op jit(solution)/shard_map/while/body/eval_jaxpr/psum | solution.py:11
  1158.4 3.0 copy-start.1
Sparse Core Ops, SparseCore 0:
  9.7 51.9 all-reduce.6
  86.4 43.9 all-reduce.8
  133.6 51.5 all-reduce.14
  188.9 52.5 all-reduce.14
  245.1 52.5 all-reduce.14
  301.4 52.5 all-reduce.14
  358.0 52.5 all-reduce.14
  414.6 52.5 all-reduce.14
  471.2 52.5 all-reduce.14
  527.5 52.5 all-reduce.14
  585.4 52.5 all-reduce.10
  662.8 44.7 all-reduce.12
  710.9 51.5 all-reduce.16
  766.2 52.5 all-reduce.16
  822.6 52.6 all-reduce.16
  879.1 52.5 all-reduce.16
  935.5 52.5 all-reduce.16
  991.9 52.5 all-reduce.16
  1048.6 52.5 all-reduce.16
  1105.0 52.5 all-reduce.16
where the time goes:
time: 1180 us; the launch traced here: 1170 us
  waiting for transfers between devices  1050 us (89%)
  other arithmetic  59.5 us (5%)
  local copies, waits for them, and re-layouts  36 us (3%)
  between operations  13.7 us (1%)
    psum x20, waiting for transfers between devices, from_root(): return lax.psum(block, axis)  1050 us
    another operation x6, other arithmetic, body(): factor_tile = jnp.linalg.cholesky(diag)  24.8 us
  transfers between devices with their start and end apart: 20, of which 20 were waited for; matrix products, arithmetic and copies ran while one was open for 0% of the time, Pallas kernels for 0%

commit v1 on v0

v1 whole, which is shorter than its diff:
```python
import functools

import jax
import jax.numpy as jnp
from jax import lax
from jax.experimental import pallas as pl
from jax.experimental.pallas import tpu as pltpu
from jax.sharding import PartitionSpec as P

MESH = pl.DeviceIdType.MESH
HIGHEST = lax.Precision.HIGHEST
CHUNKS = 4


def dot(a, b, dims):
    return lax.dot_general(
        a, b, (dims, ((), ())), precision=HIGHEST, preferred_element_type=jnp.float32
    )


NN = ((1,), (0,))
NT = ((1,), (1,))
TN = ((0,), (0,))


def invert_factor(aug):
    n = aug.shape[0]
    rows = lax.broadcasted_iota(jnp.int32, (n, n), 0)
    lanes = lax.broadcasted_iota(jnp.int32, (n, n), 1)
    aug[:, n:] = jnp.where(rows == lanes, 1.0, 0.0)
    sub = lax.broadcasted_iota(jnp.int32, (8, n), 0)
    lane = lax.broadcasted_iota(jnp.int32, (8, n), 1)

    def block(b, carry):
        base = pl.multiple_of(b * 8, 8)
        left = aug[pl.ds(base, 8), :n]
        right = aug[pl.ds(base, 8), n:]
        diag = pltpu.roll(left, n - base, 1)
        cols = [jnp.broadcast_to(diag[:, k : k + 1], (8, n)) for k in range(8)]
        scale = jnp.zeros((8, n), jnp.float32)
        for k in range(8):
            inverse = lax.rsqrt(jnp.broadcast_to(cols[k][k : k + 1], (8, n)))
            scale = jnp.where(sub == k, inverse, scale)
            if k == 7:
                break
            factor = cols[k] * inverse
            below = jnp.where(sub > k, factor, 0.0)
            for j in range(k + 1, 8):
                cols[j] = cols[j] - factor * jnp.broadcast_to(factor[j : j + 1], (8, n))
            left = left - below * (jnp.broadcast_to(left[k : k + 1], (8, n)) * inverse)
            right = right - below * (jnp.broadcast_to(right[k : k + 1], (8, n)) * inverse)
        left = left * scale
        right = right * scale
        later = jnp.where(lane >= base + 8, left, 0.0)
        aug[...] -= dot(later, jnp.concatenate([left, right], 1), TN)
        aug[pl.ds(base, 8), n:] = right
        return carry

    lax.fori_loop(0, n // 8, block, 0)


def kernel(
    rows_n, cols_n, m_ref, o_ref, row_p, col_p, first, second, corner, aug, x_s, r_s, y_s,
    send_p, recv_p, send_c, recv_c, send_w, recv_w, send_t, recv_t,
):
    r = lax.axis_index("row")
    c = lax.axis_index("col")
    tiles_r, height, width = m_ref.shape
    tiles_c = height // width
    parity = lax.rem(r, 2)
    sibling = r + 1 - 2 * parity
    root = jnp.logical_and(r == 0, c == 0)
    corner_owner = jnp.logical_and(r == 1, c == 1)

    barrier = pltpu.get_barrier_semaphore()
    for step in range(1, cols_n):
        pl.semaphore_signal(
            barrier, inc=1, device_id=(r, lax.rem(c + step, cols_n)), device_id_type=MESH
        )
    for step in range(1, rows_n):
        pl.semaphore_signal(
            barrier, inc=1, device_id=(lax.rem(r + step, rows_n), c), device_id_type=MESH
        )

    @pl.when(jnp.logical_or(root, corner_owner))
    def _():
        pl.semaphore_signal(barrier, inc=1, device_id=(1 - r, 1 - c), device_id_type=MESH)

    @pl.when(c < 2)
    def _():
        for t in range(tiles_r):
            row_p[c, t] = m_ref[t, pl.ds(0, width, stride=tiles_c), :]

    @pl.when(r < 2)
    def _():
        col_p[parity] = m_ref[0]

    on_diagonal = jnp.logical_or(root, corner_owner)

    @pl.when(on_diagonal)
    def _():
        pl.semaphore_wait(barrier, rows_n + cols_n - 1)

    @pl.when(jnp.logical_not(on_diagonal))
    def _():
        pl.semaphore_wait(barrier, rows_n + cols_n - 2)

    def send(src, dst, send_sem, recv_sem, device):
        return pltpu.make_async_remote_copy(
            src_ref=src, dst_ref=dst, send_sem=send_sem, recv_sem=recv_sem,
            device_id=device, device_id_type=MESH,
        )

    def corner_copy():
        return send(row_p.at[1, 0], corner, send_t, recv_t, (0, 0))

    def panel_copy(step):
        return send(
            row_p.at[c], row_p.at[c], send_p.at[step - 1], recv_p.at[c],
            (r, lax.rem(c + step, cols_n)),
        )

    chunk = height // CHUNKS

    def chain_copy(which, k, panel):
        part = col_p.at[panel, pl.ds(k * chunk, chunk)]
        target = (sibling, c) if which == 0 else (r + 2, c)
        return send(part, part, send_c.at[which, k], recv_c.at[panel, k], target)

    def spread_copy(phase, step, device):
        buffer = (first, second)[phase]
        return send(buffer, buffer, send_w.at[phase, step], recv_w.at[phase], device)

    pairs = rows_n // 2

    def spread(phase, act):
        @pl.when(root)
        def _():
            for step in range(1, cols_n):
                act(spread_copy(phase, step - 1, (0, step)))

        @pl.when(r == 0)
        def _():
            for step in range(1, pairs):
                act(spread_copy(phase, cols_n - 2 + step, (2 * step, c)))

        @pl.when(parity == 0)
        def _():
            act(spread_copy(phase, cols_n - 2 + pairs, (r + 1, c)))

    def wait_spread(phase):
        @pl.when(jnp.logical_not(root))
        def _():
            spread_copy(phase, 0, (sibling, c)).wait_recv()

    @pl.when(corner_owner)
    def _():
        corner_copy().start()

    @pl.when(c < 2)
    def _():
        for step in range(1, cols_n):
            panel_copy(step).start()

    for k in range(CHUNKS):
        @pl.when(r >= 2)
        def _():
            chain_copy(0, k, parity).wait_recv()

        @pl.when(r + 2 < rows_n)
        def _():
            chain_copy(1, k, parity).start()

        chain_copy(0, k, parity).start()

    def wait_panel(panel):
        @pl.when(c != panel)
        def _():
            send(
                row_p.at[panel], row_p.at[panel], send_p.at[0], recv_p.at[panel], (sibling, c)
            ).wait_recv()

    @pl.when(root)
    def _():
        aug[:, :width] = row_p[0, 0]
        invert_factor(aug)
        first[:width] = aug[:, width:]
        wait_panel(1)
        first[width:] = dot(row_p[1, 0], first[:width], ((0,), (1,)))

    @pl.when(jnp.logical_not(root))
    def _():
        wait_panel(1)

    wait_spread(0)
    spread(0, lambda copy: copy.start())

    @pl.when(root)
    def _():
        corner_copy().wait_recv()
        lower = first[width:]
        aug[:, :width] = corner[...] - dot(lower, lower, NT)
        invert_factor(aug)
        second[...] = aug[:, width:]
        spread(1, lambda copy: copy.start())

    wait_panel(0)
    for k in range(CHUNKS):
        chain_copy(0, k, 1 - parity).wait_recv()

    w0 = first[:width]
    lower = first[width:]
    last = [min(tiles_c, ((t + 1) * rows_n - 1) // cols_n + 1) for t in range(tiles_r)]
    for t in range(tiles_r):
        x0 = dot(row_p[0, t], w0, NT)
        x_s[0, t] = x0
        r_s[t] = row_p[1, t] - dot(x0, lower, NT)
    for s in range(tiles_c):
        part = pl.ds(s, width, stride=tiles_c)
        y0 = dot(w0, col_p[0, part, :], NN)
        y_s[0, s] = y0
        y_s[1, s] = col_p[1, part, :] - dot(lower, y0, NN)
    for t in range(tiles_r):
        for s in range(last[t]):
            part = pl.ds(s, width, stride=tiles_c)
            o_ref[t, part, :] = m_ref[t, part, :] - dot(x_s[0, t], y_s[0, s], NN)

    wait_spread(1)

    @pl.when(jnp.logical_not(root))
    def _():
        spread(1, lambda copy: copy.start())

    w1 = second[...]
    for t in range(tiles_r):
        x_s[1, t] = dot(r_s[t], w1, NT)
    for s in range(tiles_c):
        y_s[1, s] = dot(w1, y_s[1, s], NN)
    down = lax.broadcasted_iota(jnp.int32, (width, width), 0)
    across = lax.broadcasted_iota(jnp.int32, (width, width), 1)
    ahead = down - across
    for t in range(tiles_r):
        for s in range(tiles_c):
            part = pl.ds(s, width, stride=tiles_c)
            if s >= last[t]:
                o_ref[t, part, :] = jnp.zeros((width, width), jnp.float32)
                continue
            value = o_ref[t, part, :] - dot(x_s[1, t], y_s[1, s], NN)
            if s == 0:
                value = jnp.where(c == 0, x_s[0, t], jnp.where(c == 1, x_s[1, t], value))
            offset = ((t * rows_n + r) - (s * cols_n + c)) * width
            o_ref[t, part, :] = jnp.where(ahead + offset >= 0, value, 0.0)

    @pl.when(corner_owner)
    def _():
        corner_copy().wait_send()

    @pl.when(c < 2)
    def _():
        for step in range(1, cols_n):
            panel_copy(step).wait_send()

    for k in range(CHUNKS):
        @pl.when(r + 2 < rows_n)
        def _():
            chain_copy(1, k, parity).wait_send()

        chain_copy(0, k, parity).wait_send()
    for phase in range(2):
        spread(phase, lambda copy: copy.wait_send())


def body(matrix, rows_n, cols_n):
    tiles_r, width, tiles_c, _ = matrix.shape
    height = width * tiles_c
    spreads = cols_n - 1 + rows_n // 2
    f32 = jnp.float32
    out = pl.pallas_call(
        functools.partial(kernel, rows_n, cols_n),
        out_shape=jax.ShapeDtypeStruct((tiles_r, height, width), f32),
        in_specs=[pl.BlockSpec(memory_space=pltpu.VMEM)],
        out_specs=pl.BlockSpec(memory_space=pltpu.VMEM),
        scratch_shapes=[
            pltpu.VMEM((2, tiles_r, width, width), f32),
            pltpu.VMEM((2, height, width), f32),
            pltpu.VMEM((2 * width, width), f32),
            pltpu.VMEM((width, width), f32),
            pltpu.VMEM((width, width), f32),
            pltpu.VMEM((width, 2 * width), f32),
            pltpu.VMEM((2, tiles_r, width, width), f32),
            pltpu.VMEM((tiles_r, width, width), f32),
            pltpu.VMEM((2, tiles_c, width, width), f32),
            pltpu.SemaphoreType.DMA((cols_n - 1,)),
            pltpu.SemaphoreType.DMA((2,)),
            pltpu.SemaphoreType.DMA((2, CHUNKS)),
            pltpu.SemaphoreType.DMA((2, CHUNKS)),
            pltpu.SemaphoreType.DMA((2, spreads)),
            pltpu.SemaphoreType.DMA((2,)),
            pltpu.SemaphoreType.DMA(()),
            pltpu.SemaphoreType.DMA(()),
        ],
        compiler_params=pltpu.CompilerParams(
            collective_id=0, has_side_effects=True, vmem_limit_bytes=32 * 1024 * 1024
        ),
    )(matrix.reshape(tiles_r, height, width))
    return out.reshape(matrix.shape)


def solution(mesh):
    placed = P(None, "row", None, "col")
    return jax.shard_map(
        functools.partial(body, rows_n=mesh.shape["row"], cols_n=mesh.shape["col"]),
        mesh=mesh, in_specs=(placed,), out_specs=placed, check_vma=False,
    )
```

time: 1180 us -> 41.7 us (0.04)
  waiting for transfers between devices: 1050 us -> 0 us
  other arithmetic: 59.5 us -> 0 us
  Pallas kernels: 0 us -> 37.9 us
  local copies, waits for them, and re-layouts: 36 us -> 2.91 us
  between operations: 13.7 us -> 0.01 us
    psum x20 -> x0, waiting for transfers between devices: 1050 us -> none  [from_root(): return lax.psum(block, axis)]
    another operation x10 -> x0, other arithmetic: 45.7 us -> none  [the longest x6 24.8 us: body(): factor_tile = jnp.linalg.cholesky(diag)]
    pallas_call x0 -> x1, Pallas kernels: none -> 37.9 us  [body(): pl.pallas_call(functools.partial(kernel, rows_n, cols_n), out_shape=jax.S...]
    dynamic_slice x32 -> x0, local copies, waits for them, and re-layouts: 14.9 us -> none  [fetch(): lax.dynamic_index_in_dim(factor_row_panel, tile_id // rows_n, 0, keepdims...]
    dynamic_update_slice x16 -> x0, local copies, waits for them, and re-layouts: 13.5 us -> none  [fetch(): return lax.dynamic_update_index_in_dim(gathered, arrived, slot, 0)]
    select_n x24 -> x0, other arithmetic: 13.5 us -> none  [the longest x20 13.1 us: from_root(): jnp.where(lax.axis_index(axis) == owner, block, jnp.zeros_like(block))]
  transfers between devices with their start and end apart: 20 -> 0, of which waited for: 20 -> 0; matrix products, arithmetic and copies ran while one was open for 0% -> 0% of each run, Pallas kernels for 0% -> 0%
where the time goes in v1:
time: 41.7 us; the launch traced here: 40.8 us
  Pallas kernels  37.9 us (91%)
  local copies, waits for them, and re-layouts  2.91 us (7%)
    pallas_call x1, Pallas kernels, body(): pl.pallas_call(functools.partial(kernel, rows_n, cols_n), out_shape=jax.S...  37.9 us
    unnamed x3, local copies, waits for them, and re-layouts  2.91 us

profile of v1, /device:TPU:29, one launch (start us, length us, event | category | flops | bytes accessed | tf_op | source)
XLA Modules:
  0.0 40.8 jit_solution(675381688784282128)
XLA Ops:
  0.0 0.0 copy-start
  0.0 1.6 %copy-done = f32[4,128,8,128]{3,2,1,0:T(8,128)S(1)} copy-done((f32[4,128,8,128]{3,2,1,0:T(8,128)S(1)}, f32[4,128,8,128]{3,2,1,0:T(8,128)}, u32[]{:S(2)}) %copy-start) | copy-done | bytes 2097176
  1.6 37.9 %shard_map.17 = f32[4,1024,128]{2,1,0:T(8,128)S(1)} custom-call(f32[4,1024,128]{2,1,0:T(8,128)S(1)} %bitcast.3), custom_call_target="tpu_custom_call" | custom-call | tf_op jit(solution)/shard_map/pallas_call | solution.py:278
  39.5 1.3 %copy.3 = f32[4,128,8,128]{3,2,1,0:T(8,128)} copy(f32[4,128,8,128]{3,2,1,0:T(8,128)S(1)} %bitcast.2) | data formatting | bytes 4194304
Async XLA Ops:
  0.0 1.6 %copy-start = (f32[4,128,8,128]{3,2,1,0:T(8,128)S(1)}, f32[4,128,8,128]{3,2,1,0:T(8,128)}, u32[]{:S(2)}) copy-start(f32[4,128,8,128]{3,2,1,0:T(8,128)} %param.1) | copy-start | bytes 6291460

commit v2 on v1

--- a/solution.py
+++ b/solution.py
@@ -9,7 +9,10 @@
 
 MESH = pl.DeviceIdType.MESH
 HIGHEST = lax.Precision.HIGHEST
-CHUNKS = 4
+CHUNKS = 8
+GROUPS = 2
+PART = 2
+HEAD = 2
 
 
 def dot(a, b, dims):
@@ -23,40 +26,71 @@
 TN = ((0,), (0,))
 
 
-def invert_factor(aug):
+def split(x):
+    high = x.astype(jnp.bfloat16).astype(jnp.float32)
+    rest = x - high
+    middle = rest.astype(jnp.bfloat16).astype(jnp.float32)
+    return high, middle, rest - middle
+
+
+def outer_product(a, b):
+    a0, a1, a2 = split(a)
+    b0, b1, b2 = split(b)
+    left = jnp.concatenate([a0, a0, a1, a0, a2, a1], 0).astype(jnp.bfloat16)
+    right = jnp.concatenate([b0, b1, b0, b2, b0, b1], 0).astype(jnp.bfloat16)
+    return lax.dot_general(left, right, (TN, ((), ())), preferred_element_type=jnp.float32)
+
+
+def identity_beside(aug):
     n = aug.shape[0]
     rows = lax.broadcasted_iota(jnp.int32, (n, n), 0)
     lanes = lax.broadcasted_iota(jnp.int32, (n, n), 1)
     aug[:, n:] = jnp.where(rows == lanes, 1.0, 0.0)
+
+
+def eliminate(aug, first, last):
+    n = aug.shape[0]
     sub = lax.broadcasted_iota(jnp.int32, (8, n), 0)
-    lane = lax.broadcasted_iota(jnp.int32, (8, n), 1)
-
-    def block(b, carry):
-        base = pl.multiple_of(b * 8, 8)
-        left = aug[pl.ds(base, 8), :n]
-        right = aug[pl.ds(base, 8), n:]
-        diag = pltpu.roll(left, n - base, 1)
-        cols = [jnp.broadcast_to(diag[:, k : k + 1], (8, n)) for k in range(8)]
-        scale = jnp.zeros((8, n), jnp.float32)
-        for k in range(8):
-            inverse = lax.rsqrt(jnp.broadcast_to(cols[k][k : k + 1], (8, n)))
-            scale = jnp.where(sub == k, inverse, scale)
-            if k == 7:
+    lane = lax.broadcasted_iota(jnp.int32, (8 * GROUPS, n), 1)
+    block = 8 * GROUPS
+
+    def spread_row(x, i):
+        return jnp.broadcast_to(x[i : i + 1], (8, n))
+
+    for b in range(first, last):
+        base = b * block
+        left = [aug[base + 8 * g : base + 8 * g + 8, :n] for g in range(GROUPS)]
+        right = [aug[base + 8 * g : base + 8 * g + 8, n:] for g in range(GROUPS)]
+        cols = [
+            [jnp.broadcast_to(left[g][:, base + k : base + k + 1], (8, n)) for k in range(8 * g + 8)]
+            for g in range(GROUPS)
+        ]
+        scale = [jnp.zeros((8, n), jnp.float32) for _ in range(GROUPS)]
+        for k in range(block):
+            own, row = divmod(k, 8)
+            inverse = lax.rsqrt(spread_row(cols[own][k], row))
+            scale[own] = jnp.where(sub == row, inverse, scale[own])
+            if k == block - 1:
                 break
-            factor = cols[k] * inverse
-            below = jnp.where(sub > k, factor, 0.0)
-            for j in range(k + 1, 8):
-                cols[j] = cols[j] - factor * jnp.broadcast_to(factor[j : j + 1], (8, n))
-            left = left - below * (jnp.broadcast_to(left[k : k + 1], (8, n)) * inverse)
-            right = right - below * (jnp.broadcast_to(right[k : k + 1], (8, n)) * inverse)
-        left = left * scale
-        right = right * scale
-        later = jnp.where(lane >= base + 8, left, 0.0)
-        aug[...] -= dot(later, jnp.concatenate([left, right], 1), TN)
-        aug[pl.ds(base, 8), n:] = right
-        return carry
-
-    lax.fori_loop(0, n // 8, block, 0)
+            factor = {g: cols[g][k] * inverse for g in range(own, GROUPS)}
+            row_left = spread_row(left[own], row) * inverse
+            row_right = spread_row(right[own], row) * inverse
+            pivots = {j: spread_row(factor[j // 8], j % 8) for j in range(k + 1, block)}
+            for g in range(own, GROUPS):
+                if g == own and row == 7:
+                    continue
+                for j in range(k + 1, 8 * g + 8):
+                    cols[g][j] = cols[g][j] - factor[g] * pivots[j]
+                below = jnp.where(sub > row, factor[g], 0.0) if g == own else factor[g]
+                left[g] = left[g] - below * row_left
+                right[g] = right[g] - below * row_right
+        done_right = jnp.concatenate([right[g] * scale[g] for g in range(GROUPS)], 0)
+        if base + block < n:
+            done_left = jnp.concatenate([left[g] * scale[g] for g in range(GROUPS)], 0)
+            later = jnp.where(lane >= base + block, done_left, 0.0)
+            change = outer_product(later, jnp.concatenate([done_left, done_right], 1))
+            aug[base + block :] -= change[base + block :]
+        aug[base : base + block, n:] = done_right
 
 
 def kernel(
@@ -95,6 +129,12 @@
     def _():
         col_p[parity] = m_ref[0]
 
+    @pl.when(root)
+    def _():
+        aug[:, :width] = row_p[0, 0]
+        identity_beside(aug)
+        eliminate(aug, 0, HEAD)
+
     on_diagonal = jnp.logical_or(root, corner_owner)
 
     @pl.when(on_diagonal)
@@ -111,14 +151,21 @@
             device_id=device, device_id_type=MESH,
         )
 
-    def corner_copy():
-        return send(row_p.at[1, 0], corner, send_t, recv_t, (0, 0))
-
-    def panel_copy(step):
-        return send(
-            row_p.at[c], row_p.at[c], send_p.at[step - 1], recv_p.at[c],
-            (r, lax.rem(c + step, cols_n)),
-        )
+    def corner_copy(which):
+        return send(row_p.at[1, 0], corner.at[which], send_t, recv_t.at[which], (0, 0))
+
+    half = cols_n // 2
+
+    def panel_copy(panel, t, slot, target):
+        part = row_p.at[panel, t]
+        return send(part, part, send_p.at[panel, t, slot], recv_p.at[panel, t], (r, target))
+
+    def panels(panel, t, relay, act):
+        targets = [j for j in range(half) if j != panel] + [half + panel]
+        if relay:
+            targets = [j for j in range(half, cols_n) if j != half + panel]
+        for slot, target in enumerate(targets):
+            act(panel_copy(panel, t, slot, target))
 
     chunk = height // CHUNKS
 
@@ -153,14 +200,25 @@
         def _():
             spread_copy(phase, 0, (sibling, c)).wait_recv()
 
-    @pl.when(corner_owner)
-    def _():
-        corner_copy().start()
-
-    @pl.when(c < 2)
-    def _():
-        for step in range(1, cols_n):
-            panel_copy(step).start()
+    @pl.when(jnp.logical_and(r < 2, c == 1))
+    def _():
+        for which in range(2):
+            @pl.when(r == which)
+            def _():
+                corner_copy(which).start()
+
+    for panel in range(2):
+        @pl.when(c == panel)
+        def _():
+            for t in range(tiles_r):
+                panels(panel, t, False, lambda copy: copy.start())
+
+    def relay(t):
+        for panel in range(2):
+            @pl.when(c == half + panel)
+            def _():
+                panel_copy(panel, t, 0, 0).wait_recv()
+                panels(panel, t, True, lambda copy: copy.start())
 
     for k in range(CHUNKS):
         @pl.when(r >= 2)
@@ -172,39 +230,37 @@
             chain_copy(1, k, parity).start()
 
         chain_copy(0, k, parity).start()
+        if k % PART == 0 and k // PART < tiles_r:
+            relay(k // PART)
 
     def wait_panel(panel):
-        @pl.when(c != panel)
-        def _():
-            send(
-                row_p.at[panel], row_p.at[panel], send_p.at[0], recv_p.at[panel], (sibling, c)
-            ).wait_recv()
+        @pl.when(jnp.logical_and(c != panel, c != half + panel))
+        def _():
+            for t in range(tiles_r):
+                panel_copy(panel, t, 0, 0).wait_recv()
 
     @pl.when(root)
     def _():
-        aug[:, :width] = row_p[0, 0]
-        invert_factor(aug)
+        eliminate(aug, HEAD, width // (8 * GROUPS))
         first[:width] = aug[:, width:]
-        wait_panel(1)
-        first[width:] = dot(row_p[1, 0], first[:width], ((0,), (1,)))
-
-    @pl.when(jnp.logical_not(root))
-    def _():
-        wait_panel(1)
+        corner_copy(0).wait_recv()
+        first[width:] = dot(corner[0], first[:width], ((0,), (1,)))
 
     wait_spread(0)
     spread(0, lambda copy: copy.start())
 
     @pl.when(root)
     def _():
-        corner_copy().wait_recv()
+        corner_copy(1).wait_recv()
         lower = first[width:]
-        aug[:, :width] = corner[...] - dot(lower, lower, NT)
-        invert_factor(aug)
+        aug[:, :width] = corner[1] - dot(lower, lower, NT)
+        identity_beside(aug)
+        eliminate(aug, 0, width // (8 * GROUPS))
         second[...] = aug[:, width:]
         spread(1, lambda copy: copy.start())
 
     wait_panel(0)
+    wait_panel(1)
     for k in range(CHUNKS):
         chain_copy(0, k, 1 - parity).wait_recv()
 
@@ -251,14 +307,16 @@
             offset = ((t * rows_n + r) - (s * cols_n + c)) * width
             o_ref[t, part, :] = jnp.where(ahead + offset >= 0, value, 0.0)
 
-    @pl.when(corner_owner)
-    def _():
-        corner_copy().wait_send()
-
-    @pl.when(c < 2)
-    def _():
-        for step in range(1, cols_n):
-            panel_copy(step).wait_send()
+    @pl.when(jnp.logical_and(r < 2, c == 1))
+    def _():
+        corner_copy(0).wait_send()
+
+    for panel in range(2):
+        for t in range(tiles_r):
+            for owner, passed_on in ((panel, False), (half + panel, True)):
+                @pl.when(c == owner)
+                def _():
+                    panels(panel, t, passed_on, lambda copy: copy.wait_send())
 
     for k in range(CHUNKS):
         @pl.when(r + 2 < rows_n)
@@ -285,19 +343,19 @@
             pltpu.VMEM((2, height, width), f32),
             pltpu.VMEM((2 * width, width), f32),
             pltpu.VMEM((width, width), f32),
-            pltpu.VMEM((width, width), f32),
+            pltpu.VMEM((2, width, width), f32),
             pltpu.VMEM((width, 2 * width), f32),
             pltpu.VMEM((2, tiles_r, width, width), f32),
             pltpu.VMEM((tiles_r, width, width), f32),
             pltpu.VMEM((2, tiles_c, width, width), f32),
-            pltpu.SemaphoreType.DMA((cols_n - 1,)),
-            pltpu.SemaphoreType.DMA((2,)),
+            pltpu.SemaphoreType.DMA((2, tiles_r, max(cols_n // 2, 1))),
+            pltpu.SemaphoreType.DMA((2, tiles_r)),
             pltpu.SemaphoreType.DMA((2, CHUNKS)),
             pltpu.SemaphoreType.DMA((2, CHUNKS)),
             pltpu.SemaphoreType.DMA((2, spreads)),
             pltpu.SemaphoreType.DMA((2,)),
             pltpu.SemaphoreType.DMA(()),
-            pltpu.SemaphoreType.DMA(()),
+            pltpu.SemaphoreType.DMA((2,)),
         ],
         compiler_params=pltpu.CompilerParams(
             collective_id=0, has_side_effects=True, vmem_limit_bytes=32 * 1024 * 1024

time: 41.7 us -> 41.4 us (level); the launches traced: 40.8 us -> 41.2 us
  no operation moved by 1% of the time
where the time goes in v2:
time: 41.4 us; the launch traced here: 41.2 us
  Pallas kernels  38.3 us (93%)
  local copies, waits for them, and re-layouts  2.91 us (7%)
    pallas_call x1, Pallas kernels, body(): pl.pallas_call(functools.partial(kernel, rows_n, cols_n), out_shape=jax.S...  38.3 us
    unnamed x3, local copies, waits for them, and re-layouts  2.91 us

profile of v2, /device:TPU:29, one launch (start us, length us, event | category | flops | bytes accessed | tf_op | source)
XLA Modules:
  0.0 41.2 jit_solution(16608338500093481898)
XLA Ops:
  0.0 0.0 copy-start
  0.0 1.6 %copy-done = f32[4,128,8,128]{3,2,1,0:T(8,128)S(1)} copy-done((f32[4,128,8,128]{3,2,1,0:T(8,128)S(1)}, f32[4,128,8,128]{3,2,1,0:T(8,128)}, u32[]{:S(2)}) %copy-start) | copy-done | bytes 2097176
  1.6 38.3 %shard_map.17 = f32[4,1024,128]{2,1,0:T(8,128)S(1)} custom-call(f32[4,1024,128]{2,1,0:T(8,128)S(1)} %bitcast.3), custom_call_target="tpu_custom_call" | custom-call | tf_op jit(solution)/shard_map/pallas_call | solution.py:336
  39.9 1.3 %copy.3 = f32[4,128,8,128]{3,2,1,0:T(8,128)} copy(f32[4,128,8,128]{3,2,1,0:T(8,128)S(1)} %bitcast.2) | data formatting | bytes 4194304
Async XLA Ops:
  0.0 1.6 %copy-start = (f32[4,128,8,128]{3,2,1,0:T(8,128)S(1)}, f32[4,128,8,128]{3,2,1,0:T(8,128)}, u32[]{:S(2)}) copy-start(f32[4,128,8,128]{3,2,1,0:T(8,128)} %param.1) | copy-start | bytes 6291460

commit v3 on v2

--- a/solution.py
+++ b/solution.py
@@ -9,9 +9,7 @@
 
 MESH = pl.DeviceIdType.MESH
 HIGHEST = lax.Precision.HIGHEST
-CHUNKS = 8
 GROUPS = 2
-PART = 2
 HEAD = 2
 
 
@@ -127,7 +125,8 @@
 
     @pl.when(r < 2)
     def _():
-        col_p[parity] = m_ref[0]
+        for s in range(tiles_c):
+            col_p[parity, s] = m_ref[0, pl.ds(s, width, stride=tiles_c), :]
 
     @pl.when(root)
     def _():
@@ -167,10 +166,8 @@
         for slot, target in enumerate(targets):
             act(panel_copy(panel, t, slot, target))
 
-    chunk = height // CHUNKS
-
     def chain_copy(which, k, panel):
-        part = col_p.at[panel, pl.ds(k * chunk, chunk)]
+        part = col_p.at[panel, k]
         target = (sibling, c) if which == 0 else (r + 2, c)
         return send(part, part, send_c.at[which, k], recv_c.at[panel, k], target)
 
@@ -220,7 +217,7 @@
                 panel_copy(panel, t, 0, 0).wait_recv()
                 panels(panel, t, True, lambda copy: copy.start())
 
-    for k in range(CHUNKS):
+    def pass_on(k):
         @pl.when(r >= 2)
         def _():
             chain_copy(0, k, parity).wait_recv()
@@ -230,14 +227,23 @@
             chain_copy(1, k, parity).start()
 
         chain_copy(0, k, parity).start()
-        if k % PART == 0 and k // PART < tiles_r:
-            relay(k // PART)
+    ahead_by = max(tiles_c // 2, 1)
+    for k in range(max(ahead_by, tiles_r)):
+        if k < tiles_r:
+            relay(k)
+        if k < ahead_by:
+            pass_on(k)
 
     def wait_panel(panel):
         @pl.when(jnp.logical_and(c != panel, c != half + panel))
         def _():
             for t in range(tiles_r):
                 panel_copy(panel, t, 0, 0).wait_recv()
+
+    @pl.when(r < 2)
+    def _():
+        for k in range(ahead_by, tiles_c):
+            pass_on(k)
 
     @pl.when(root)
     def _():
@@ -261,9 +267,6 @@
 
     wait_panel(0)
     wait_panel(1)
-    for k in range(CHUNKS):
-        chain_copy(0, k, 1 - parity).wait_recv()
-
     w0 = first[:width]
     lower = first[width:]
     last = [min(tiles_c, ((t + 1) * rows_n - 1) // cols_n + 1) for t in range(tiles_r)]
@@ -272,14 +275,19 @@
         x_s[0, t] = x0
         r_s[t] = row_p[1, t] - dot(x0, lower, NT)
     for s in range(tiles_c):
+        if s + ahead_by < tiles_c:
+            @pl.when(r >= 2)
+            def _():
+                pass_on(s + ahead_by)
+
+        chain_copy(0, s, 1 - parity).wait_recv()
         part = pl.ds(s, width, stride=tiles_c)
-        y0 = dot(w0, col_p[0, part, :], NN)
+        y0 = dot(w0, col_p[0, s], NN)
         y_s[0, s] = y0
-        y_s[1, s] = col_p[1, part, :] - dot(lower, y0, NN)
-    for t in range(tiles_r):
-        for s in range(last[t]):
-            part = pl.ds(s, width, stride=tiles_c)
-            o_ref[t, part, :] = m_ref[t, part, :] - dot(x_s[0, t], y_s[0, s], NN)
+        y_s[1, s] = col_p[1, s] - dot(lower, y0, NN)
+        for t in range(tiles_r):
+            if s < last[t]:
+                o_ref[t, part, :] = m_ref[t, part, :] - dot(x_s[0, t], y0, NN)
 
     wait_spread(1)
 
@@ -318,7 +326,7 @@
                 def _():
                     panels(panel, t, passed_on, lambda copy: copy.wait_send())
 
-    for k in range(CHUNKS):
+    for k in range(tiles_c):
         @pl.when(r + 2 < rows_n)
         def _():
             chain_copy(1, k, parity).wait_send()
@@ -340,7 +348,7 @@
         out_specs=pl.BlockSpec(memory_space=pltpu.VMEM),
         scratch_shapes=[
             pltpu.VMEM((2, tiles_r, width, width), f32),
-            pltpu.VMEM((2, height, width), f32),
+            pltpu.VMEM((2, tiles_c, width, width), f32),
             pltpu.VMEM((2 * width, width), f32),
             pltpu.VMEM((width, width), f32),
             pltpu.VMEM((2, width, width), f32),
@@ -350,8 +358,8 @@
             pltpu.VMEM((2, tiles_c, width, width), f32),
             pltpu.SemaphoreType.DMA((2, tiles_r, max(cols_n // 2, 1))),
             pltpu.SemaphoreType.DMA((2, tiles_r)),
-            pltpu.SemaphoreType.DMA((2, CHUNKS)),
-            pltpu.SemaphoreType.DMA((2, CHUNKS)),
+            pltpu.SemaphoreType.DMA((2, tiles_c)),
+            pltpu.SemaphoreType.DMA((2, tiles_c)),
             pltpu.SemaphoreType.DMA((2, spreads)),
             pltpu.SemaphoreType.DMA((2,)),
             pltpu.SemaphoreType.DMA(()),

time: 41.4 us -> 44.8 us (1.082)
  Pallas kernels: 38.3 us -> 41.7 us
    pallas_call x1, Pallas kernels: 38.3 us -> 41.7 us  [body(): pl.pallas_call(functools.partial(kernel, rows_n, cols_n), out_shape=jax.S...]
where the time goes in v3:
time: 44.8 us; the launch traced here: 44.7 us
  Pallas kernels  41.7 us (93%)
  local copies, waits for them, and re-layouts  2.91 us (6%)
    pallas_call x1, Pallas kernels, body(): pl.pallas_call(functools.partial(kernel, rows_n, cols_n), out_shape=jax.S...  41.7 us
    unnamed x3, local copies, waits for them, and re-layouts  2.91 us

profile of v3, /device:TPU:29, one launch (start us, length us, event | category | flops | bytes accessed | tf_op | source)
XLA Modules:
  0.0 44.7 jit_solution(9031869402150208860)
XLA Ops:
  0.0 0.0 copy-start
  0.0 1.6 %copy-done = f32[4,128,8,128]{3,2,1,0:T(8,128)S(1)} copy-done((f32[4,128,8,128]{3,2,1,0:T(8,128)S(1)}, f32[4,128,8,128]{3,2,1,0:T(8,128)}, u32[]{:S(2)}) %copy-start) | copy-done | bytes 2097176
  1.6 41.7 %shard_map.17 = f32[4,1024,128]{2,1,0:T(8,128)S(1)} custom-call(f32[4,1024,128]{2,1,0:T(8,128)S(1)} %bitcast.3), custom_call_target="tpu_custom_call" | custom-call | tf_op jit(solution)/shard_map/pallas_call | solution.py:344
  43.3 1.3 %copy.3 = f32[4,128,8,128]{3,2,1,0:T(8,128)} copy(f32[4,128,8,128]{3,2,1,0:T(8,128)S(1)} %bitcast.2) | data formatting | bytes 4194304
Async XLA Ops:
  0.0 1.6 %copy-start = (f32[4,128,8,128]{3,2,1,0:T(8,128)S(1)}, f32[4,128,8,128]{3,2,1,0:T(8,128)}, u32[]{:S(2)}) copy-start(f32[4,128,8,128]{3,2,1,0:T(8,128)} %param.1) | copy-start | bytes 6291460

commit v4 on v3

--- a/solution.py
+++ b/solution.py
@@ -17,6 +17,16 @@
     return lax.dot_general(
         a, b, (dims, ((), ())), precision=HIGHEST, preferred_element_type=jnp.float32
     )
+
+
+def product(a, b):
+    a0 = a.astype(jnp.bfloat16)
+    a1 = (a - a0.astype(jnp.float32)).astype(jnp.bfloat16)
+    b0 = b.astype(jnp.bfloat16)
+    b1 = (b - b0.astype(jnp.float32)).astype(jnp.bfloat16)
+    left = jnp.concatenate([a0, a0, a1], 1)
+    right = jnp.concatenate([b0, b1, b0], 0)
+    return lax.dot_general(left, right, (NN, ((), ())), preferred_element_type=jnp.float32)
 
 
 NN = ((1,), (0,))
@@ -227,23 +237,17 @@
             chain_copy(1, k, parity).start()
 
         chain_copy(0, k, parity).start()
-    ahead_by = max(tiles_c // 2, 1)
-    for k in range(max(ahead_by, tiles_r)):
+    for k in range(max(tiles_c, tiles_r)):
+        if k < tiles_c:
+            pass_on(k)
         if k < tiles_r:
             relay(k)
-        if k < ahead_by:
-            pass_on(k)
 
     def wait_panel(panel):
         @pl.when(jnp.logical_and(c != panel, c != half + panel))
         def _():
             for t in range(tiles_r):
                 panel_copy(panel, t, 0, 0).wait_recv()
-
-    @pl.when(r < 2)
-    def _():
-        for k in range(ahead_by, tiles_c):
-            pass_on(k)
 
     @pl.when(root)
     def _():
@@ -275,11 +279,6 @@
         x_s[0, t] = x0
         r_s[t] = row_p[1, t] - dot(x0, lower, NT)
     for s in range(tiles_c):
-        if s + ahead_by < tiles_c:
-            @pl.when(r >= 2)
-            def _():
-                pass_on(s + ahead_by)
-
         chain_copy(0, s, 1 - parity).wait_recv()
         part = pl.ds(s, width, stride=tiles_c)
         y0 = dot(w0, col_p[0, s], NN)
@@ -287,7 +286,7 @@
         y_s[1, s] = col_p[1, s] - dot(lower, y0, NN)
         for t in range(tiles_r):
             if s < last[t]:
-                o_ref[t, part, :] = m_ref[t, part, :] - dot(x_s[0, t], y0, NN)
+                o_ref[t, part, :] = m_ref[t, part, :] - product(x_s[0, t], y0)
 
     wait_spread(1)
 
@@ -309,7 +308,7 @@
             if s >= last[t]:
                 o_ref[t, part, :] = jnp.zeros((width, width), jnp.float32)
                 continue
-            value = o_ref[t, part, :] - dot(x_s[1, t], y_s[1, s], NN)
+            value = o_ref[t, part, :] - product(x_s[1, t], y_s[1, s])
             if s == 0:
                 value = jnp.where(c == 0, x_s[0, t], jnp.where(c == 1, x_s[1, t], value))
             offset = ((t * rows_n + r) - (s * cols_n + c)) * width

time: 44.8 us -> 40.6 us (0.906)
  Pallas kernels: 41.7 us -> 37.5 us
    pallas_call x1, Pallas kernels: 41.7 us -> 37.5 us  [body(): pl.pallas_call(functools.partial(kernel, rows_n, cols_n), out_shape=jax.S...]
where the time goes in v4:
time: 40.6 us; the launch traced here: 40.4 us
  Pallas kernels  37.5 us (92%)
  local copies, waits for them, and re-layouts  2.91 us (7%)
    pallas_call x1, Pallas kernels, body(): pl.pallas_call(functools.partial(kernel, rows_n, cols_n), out_shape=jax.S...  37.5 us
    unnamed x3, local copies, waits for them, and re-layouts  2.91 us

profile of v4, /device:TPU:29, one launch (start us, length us, event | category | flops | bytes accessed | tf_op | source)
XLA Modules:
  0.0 40.4 jit_solution(5022402510671681317)
XLA Ops:
  0.0 0.0 copy-start
  0.0 1.6 %copy-done = f32[4,128,8,128]{3,2,1,0:T(8,128)S(1)} copy-done((f32[4,128,8,128]{3,2,1,0:T(8,128)S(1)}, f32[4,128,8,128]{3,2,1,0:T(8,128)}, u32[]{:S(2)}) %copy-start) | copy-done | bytes 2097176
  1.6 37.5 %shard_map.17 = f32[4,1024,128]{2,1,0:T(8,128)S(1)} custom-call(f32[4,1024,128]{2,1,0:T(8,128)S(1)} %bitcast.3), custom_call_target="tpu_custom_call" | custom-call | tf_op jit(solution)/shard_map/pallas_call | solution.py:343
  39.1 1.3 %copy.3 = f32[4,128,8,128]{3,2,1,0:T(8,128)} copy(f32[4,128,8,128]{3,2,1,0:T(8,128)S(1)} %bitcast.2) | data formatting | bytes 4194304
Async XLA Ops:
  0.0 1.6 %copy-start = (f32[4,128,8,128]{3,2,1,0:T(8,128)S(1)}, f32[4,128,8,128]{3,2,1,0:T(8,128)}, u32[]{:S(2)}) copy-start(f32[4,128,8,128]{3,2,1,0:T(8,128)} %param.1) | copy-start | bytes 6291460
